TPU v7x, 256 devices: a whole 4x4x8 slice. The times are simulated.
256 devices in a mesh: row: 2 (over core), col: 16 (over y, x), depth: 8 (over z).
Axes of the slice: x: 4, y: 4, z: 8, core: 2. Of those that a mesh axis runs over, the one named last changes fastest.
Arguments:
- tokens_in: bfloat16 [8192, 2560], P(('row', 'depth'), 'col'), may hold values from -6 to 6
- w_in: bfloat16 [2560, 10240], P('row', 'col'), may hold values from -0.15625 to 0.15625
- w_out: bfloat16 [2560, 10240], P('row', 'col'), may hold values from -0.078125 to 0.078125
- grad_out: bfloat16 [8192, 2560], P(('row', 'depth'), 'col'), may hold values from -3 to 3
Outputs:
- block_out: bfloat16 [8192, 2560], P(('row', 'depth'), 'col')
- grad_tokens: bfloat16 [8192, 2560], P(('row', 'depth'), 'col')
- grad_w_in: bfloat16 [2560, 10240], P('row', 'col')
- grad_w_out: bfloat16 [2560, 10240], P('row', 'col')
All inputs are finite; a program needn't handle non-finite values.
Results may differ from a plain program's by a relative error of at most 0.023.
Values may be sent and summed in bfloat16 or wider, within the bound.
A program may use at most 128 MiB of HBM per device.

v0:
```python
import jax
import jax.numpy as jnp
from jax import lax
from jax.sharding import PartitionSpec as P


def gelu_tanh(value):
    return jax.nn.gelu(value, approximate=True)


def times_transposed(left, right):
    return lax.dot_general(
        left, right, (((1,), (1,)), ((), ())), preferred_element_type=jnp.float32
    )


def body(tokens_in, w_in, w_out, grad_out):
    hidden_cols = w_in.shape[1]
    full_tokens = lax.all_gather(tokens_in, "col", axis=1, tiled=True)
    full_grads = lax.all_gather(grad_out, "col", axis=1, tiled=True)
    in_columns, out_columns = (
        lax.all_gather(w_in, "row", axis=0, tiled=True),
        lax.all_gather(w_out, "row", axis=0, tiled=True),
    )
    pre = jnp.dot(full_tokens, in_columns, preferred_element_type=jnp.float32)
    hidden = gelu_tanh(pre).astype(jnp.bfloat16)
    out_terms = times_transposed(hidden, out_columns)
    block_out = lax.psum_scatter(
        out_terms.astype(jnp.bfloat16), "col", scatter_dimension=1, tiled=True
    )
    grad_hidden = jnp.dot(full_grads, out_columns, preferred_element_type=jnp.float32)
    _, pullback = jax.vjp(gelu_tanh, pre)
    grad_pre = pullback(grad_hidden)[0].astype(jnp.bfloat16)
    input_terms = times_transposed(grad_pre, in_columns)
    grad_tokens = lax.psum_scatter(
        input_terms.astype(jnp.bfloat16), "col", scatter_dimension=1, tiled=True
    )
    first = lax.dot_general(
        full_tokens, grad_pre, (((0,), (0,)), ((), ())), preferred_element_type=jnp.float32
    )
    second = lax.dot_general(
        full_grads, hidden, (((0,), (0,)), ((), ())), preferred_element_type=jnp.float32
    )
    summed = lax.psum_scatter(
        jnp.concatenate([first, second], axis=1).astype(jnp.bfloat16),
        ("row", "depth"),
        scatter_dimension=0,
        tiled=True,
    )
    both_grads = lax.all_gather(summed, "depth", axis=0, tiled=True)
    grad_w_in = both_grads[:, :hidden_cols]
    grad_w_out = both_grads[:, hidden_cols:]
    return (block_out, grad_tokens, grad_w_in, grad_w_out)


def solution(mesh):
    placed = (
        P(("row", "depth"), "col"),
        P("row", "col"),
        P("row", "col"),
        P(("row", "depth"), "col"),
    )
    return jax.shard_map(
        body,
        mesh=mesh,
        in_specs=placed,
        out_specs=(
            P(("row", "depth"), "col"),
            P(("row", "depth"), "col"),
            P("row", "col"),
            P("row", "col"),
        ),
        check_vma=False,
    )
```

profile of v0, /device:TPU:1, one launch (start us, length us, event | category | flops | bytes accessed | tf_op | source)
XLA Modules:
  0.0 486.5 jit_solution(2232497447023871437)
XLA Ops:
  7.2 0.0 all-gather.10.cloned.1.call-start
  7.2 0.7 all-gather.10.cloned.1.call-update
  7.9 0.0 all-gather.12.cloned.1.call-start
  7.9 0.7 all-gather.12.cloned.1.call-update
  8.6 0.0 all-gather.8.cloned.1.call-start
  8.7 0.7 all-gather.8.cloned.1.call-update
  9.4 0.0 all-gather.6.cloned.1.call-start
  9.4 0.5 all-gather.6.cloned.1.call-update
  10.0 0.0 reduce-scatter.10.cloned.1.call-start
  10.0 22.0 %all-gather.10.cloned.1.call-done = bf16[2560,640]{1,0:T(8,128)(2,1)} async-done(((bf16[1280,640]{1,0:T(8,128)(2,1)}), bf16[2560,640]{1,0:T(8,128)(2,1)}) %all-gather.10.cloned.1.call-update) | async-done | bytes 3276816 | tf_op jit(solution)/shard_map/all_gather | solution.py:23
  32.0 54.0 %all-gather.12.cloned.1.call-done = bf16[512,2560]{0,1:T(8,128)(2,1)} async-done(((bf16[512,160]{0,1:T(8,128)(2,1)}), bf16[512,2560]{0,1:T(8,128)(2,1)}) %all-gather.12.cloned.1.call-update) | async-done | bytes 2621456 | tf_op jit(solution)/shard_map/all_gather | solution.py:20
  86.0 5.0 %fusion.10 = f32[512,640]{1,0:T(8,128)S(1)} fusion(bf16[512,2560]{0,1:T(8,128)(2,1)} %all-gather.12.cloned.1.call-done, bf16[2560,640]{1,0:T(8,128)(2,1)} %all-gather.10.cloned.1.call-done), kind=kOutput, calls=%fused_computation.18 | convolution fusion | flops 1677721600 | bytes 7208960 | tf_op jit(solution)/shard_map/dot_general | solution.py:31
  90.9 15.0 %all-gather.8.cloned.1.call-done = bf16[2560,640]{1,0:T(8,128)(2,1)} async-done(((bf16[1280,640]{1,0:T(8,128)(2,1)}), bf16[2560,640]{1,0:T(8,128)(2,1)}) %all-gather.8.cloned.1.call-update) | async-done | bytes 3276816 | tf_op jit(solution)/shard_map/all_gather | solution.py:22
  105.9 53.8 %all-gather.6.cloned.1.call-done = bf16[512,2560]{0,1:T(8,128)(2,1)} async-done(((bf16[512,160]{0,1:T(8,128)(2,1)}), bf16[512,2560]{0,1:T(8,128)(2,1)}) %all-gather.6.cloned.1.call-update) | async-done | bytes 2621456 | tf_op jit(solution)/shard_map/all_gather | solution.py:19
  159.8 0.0 copy-start.2
  159.8 5.8 %fusion.8 = (bf16[512,640]{1,0:T(8,128)(2,1)S(1)}, f32[512,640]{1,0:T(8,128)S(1)}) fusion(f32[512,640]{1,0:T(8,128)S(1)} %fusion.10, bf16[512,2560]{0,1:T(8,128)(2,1)} %all-gather.6.cloned.1.call-done, bf16[2560,640]{1,0:T(8,128)(2,1)} %all-gather.8.cloned.1.call-done), kind=kOutput, calls=%fused_computation.15 | convolution fusion | flops 1684275200 | bytes 9175040 | tf_op jit(solution)/shard_map/dot_general | solution.py:25
  165.6 0.0 copy-start.4
  165.6 0.0 copy-start.3
  165.6 0.0 copy-done.2
  165.6 0.0 copy-start.1
  165.6 1.9 fusion
  167.6 0.0 copy-done.4
  167.6 0.0 copy-done.3
  167.6 0.5 copy-done.1
  168.0 2.0 fusion.1
  170.1 3.2 pad_maximum_fusion
  173.3 9.4 %copy.11 = bf16[2560,1280]{1,0:T(8,128)(2,1)} copy(bf16[2560,1280]{0,1:T(8,128)(2,1)} %pad_maximum_fusion) | data formatting | bytes 13107200
  182.7 0.0 reduce-scatter.10.cloned.1.call-update
  182.7 0.0 all-gather.14.cloned.1.call-start
  182.8 82.8 %reduce-scatter.10.cloned.1.call-done = bf16[160,1280]{1,0:T(8,128)(2,1)} async-done(((bf16[2560,1280]{1,0:T(8,128)(2,1)}), bf16[160,1280]{1,0:T(8,128)(2,1)}) %reduce-scatter.10.cloned.1.call-update) | async-done | bytes 409616 | tf_op jit(solution)/shard_map/reduce_scatter | solution.py:44
  265.6 0.0 all-gather.14.cloned.1.call-update
  265.6 0.0 reduce-scatter.8.cloned.1.call-start
  265.7 0.0 copy-start
  265.7 6.0 %convolution_convert_fusion.2 = bf16[512,2560]{0,1:T(8,128)(2,1)} fusion(bf16[512,640]{1,0:T(8,128)(2,1)} %copy-done.4, bf16[2560,640]{1,0:T(8,128)(2,1)} %all-gather.8.cloned.1.call-done), kind=kOutput, calls=%fused_computation.3 | convolution fusion | flops 1679032320 | bytes 6553600 | tf_op jit(solution)/shard_map/dot_general | solution.py:12
  271.7 0.0 reduce-scatter.8.cloned.1.call-update
  271.7 0.2 reduce-scatter.6.cloned.1.call-start
  272.0 0.0 copy-done
  272.0 5.2 %convolution_convert_fusion.3 = bf16[512,2560]{0,1:T(8,128)(2,1)} fusion(bf16[2560,640]{1,0:T(8,128)(2,1)S(1)} %copy-done, f32[512,640]{1,0:T(8,128)} %copy-done.3), kind=kOutput, calls=%fused_computation.4 | convolution fusion | flops 1681981440 | bytes 7208960 | tf_op jit(solution)/shard_map/dot_general | solution.py:12
  277.2 0.0 reduce-scatter.6.cloned.1.call-update
  277.2 36.5 %all-gather.14.cloned.1.call-done = bf16[1280,1280]{1,0:T(8,128)(2,1)} async-done(((bf16[160,1280]{1,0:T(8,128)(2,1)}), bf16[1280,1280]{1,0:T(8,128)(2,1)}) %all-gather.14.cloned.1.call-update) | async-done | bytes 3276816 | tf_op jit(solution)/shard_map/all_gather | solution.py:50
  313.8 3.9 fusion.9
  317.7 77.8 %reduce-scatter.8.cloned.1.call-done = bf16[512,160]{0,1:T(8,128)(2,1)} async-done(((bf16[512,2560]{0,1:T(8,128)(2,1)}), bf16[512,160]{0,1:T(8,128)(2,1)}) %reduce-scatter.8.cloned.1.call-update) | async-done | bytes 163856 | tf_op jit(solution)/shard_map/reduce_scatter | solution.py:35
  395.5 84.2 %reduce-scatter.6.cloned.1.call-done = bf16[512,160]{0,1:T(8,128)(2,1)} async-done(((bf16[512,2560]{0,1:T(8,128)(2,1)}), bf16[512,160]{0,1:T(8,128)(2,1)}) %reduce-scatter.6.cloned.1.call-update) | async-done | bytes 163856 | tf_op jit(solution)/shard_map/reduce_scatter | solution.py:28
Async XLA Ops:
  7.2 24.9 %all-gather.10.cloned.1.call-start = ((), (), s32[]{:S(2)}) async-start(), calls=%async_computation.5 | async-start | bytes 4915200 | tf_op jit(solution)/shard_map/all_gather | solution.py:23
  7.9 78.1 %all-gather.12.cloned.1.call-start = ((), (), s32[]{:S(2)}) async-start(), calls=%async_computation.7 | async-start | bytes 2785280 | tf_op jit(solution)/shard_map/all_gather | solution.py:20
  8.6 97.3 %all-gather.8.cloned.1.call-start = ((), (), s32[]{:S(2)}) async-start(), calls=%async_computation.4 | async-start | bytes 4915200 | tf_op jit(solution)/shard_map/all_gather | solution.py:22
  9.4 150.4 %all-gather.6.cloned.1.call-start = ((), (), s32[]{:S(2)}) async-start(), calls=%async_computation.3 | async-start | bytes 2785280 | tf_op jit(solution)/shard_map/all_gather | solution.py:19
  10.0 255.6 %reduce-scatter.10.cloned.1.call-start = ((), (), s32[]{:S(2)}) async-start(), calls=%async_computation.10 | async-start | bytes 6963200 | tf_op jit(solution)/shard_map/reduce_scatter | solution.py:44
  159.8 5.8 %copy-start.2 = (bf16[512,2560]{0,1:T(8,128)(2,1)S(1)}, bf16[512,2560]{0,1:T(8,128)(2,1)}, u32[]{:S(2)}) copy-start(bf16[512,2560]{0,1:T(8,128)(2,1)} %all-gather.6.cloned.1.call-done) | copy-start | bytes 7864324
  165.6 2.0 copy-start.4
  165.6 2.0 copy-start.3
  165.6 2.4 copy-start.1
  182.7 131.0 %all-gather.14.cloned.1.call-start = ((), (), s32[]{:S(2)}) async-start(), calls=%async_computation.9 | async-start | bytes 3686400 | tf_op jit(solution)/shard_map/all_gather | solution.py:50
  265.6 129.8 %reduce-scatter.8.cloned.1.call-start = ((), (), s32[]{:S(2)}) async-start(), calls=%async_computation.8 | async-start | bytes 2785280 | tf_op jit(solution)/shard_map/reduce_scatter | solution.py:35
  265.7 6.3 %copy-start = (bf16[2560,640]{1,0:T(8,128)(2,1)S(1)}, bf16[2560,640]{1,0:T(8,128)(2,1)}, u32[]{:S(2)}) copy-start(bf16[2560,640]{1,0:T(8,128)(2,1)} %all-gather.10.cloned.1.call-done) | copy-start | bytes 9830404
  271.7 207.9 %reduce-scatter.6.cloned.1.call-start = ((), (), s32[]{:S(2)}) async-start(), calls=%async_computation.6 | async-start | bytes 2785280 | tf_op jit(solution)/shard_map/reduce_scatter | solution.py:28
Sparse Core Ops, SparseCore 0:
  9.8 22.1 all-gather.9
  34.4 51.4 all-gather.11
  87.8 18.1 all-gather.7
  108.2 51.4 all-gather.5
  182.9 82.6 reduce-scatter.9
  267.4 46.3 all-gather.13
  318.4 77.0 reduce-scatter.7
  400.1 79.5 reduce-scatter.5
where the time goes:
time: 487 us; the launch traced here: 486 us
  waiting for transfers between devices  429 us (88%)
  matrix products  26 us (5%)
  between operations  14.2 us (3%)
  local copies, waits for them, and re-layouts  13.8 us (3%)
    reduce_scatter x1, waiting for transfers between devices, body(): lax.psum_scatter(out_terms.astype(jnp.bfloat16), 'col', scatter_dimension...  84.2 us
    reduce_scatter x1, waiting for transfers between devices, body(): lax.psum_scatter(jnp.concatenate([first, second], axis=1).astype(jnp.bflo...  82.8 us
    reduce_scatter x1, waiting for transfers between devices, body(): lax.psum_scatter(input_terms.astype(jnp.bfloat16), 'col', scatter_dimensi...  77.8 us
    all_gather x1, waiting for transfers between devices, body(): full_grads = lax.all_gather(grad_out, 'col', axis=1, tiled=True)  54 us
    all_gather x1, waiting for transfers between devices, body(): full_tokens = lax.all_gather(tokens_in, 'col', axis=1, tiled=True)  53.8 us
    all_gather x1, waiting for transfers between devices, body(): both_grads = lax.all_gather(summed, 'depth', axis=0, tiled=True)  36.5 us
    all_gather x1, waiting for transfers between devices, body(): lax.all_gather(w_out, 'row', axis=0, tiled=True)  22 us
    all_gather x1, waiting for transfers between devices, body(): lax.all_gather(w_in, 'row', axis=0, tiled=True)  15 us
  transfers between devices with their start and end apart: 8, of which 8 were waited for; matrix products, arithmetic and copies ran while one was open for 4% of the time, Pallas kernels for 0%

commit v1 on v0

v1 whole, which is shorter than its diff:
```python
import functools

import jax
import jax.numpy as jnp
from jax import lax
from jax.experimental import pallas as pl
from jax.experimental.pallas import tpu as pltpu
from jax.sharding import PartitionSpec as P

MESH = pl.DeviceIdType.MESH
F32 = jnp.float32
BF16 = jnp.bfloat16
C0 = 0.7978845608028654
C1 = 0.044715


def nt(left, right):
    return lax.dot_general(left, right, (((1,), (1,)), ((), ())), preferred_element_type=F32)


def nn(left, right):
    return jnp.dot(left, right, preferred_element_type=F32)


class Copies:
    def __init__(self, send, recv):
        self.send, self.recv, self.count, self.sent = send, recv, 0, []

    def make(self, src, dst, device):
        k = self.count
        self.count += 1
        return pltpu.make_async_remote_copy(
            src_ref=src,
            dst_ref=dst,
            send_sem=self.send.at[k],
            recv_sem=self.recv.at[k],
            device_id=device,
            device_id_type=MESH,
        )

    def start(self, src, dst, device):
        copy = self.make(src, dst, device)
        copy.start()
        self.sent.append(copy)
        return copy


def kernel(
    tok_ref, grd_ref, win_ref, wout_ref,
    outT_ref, gtokT_ref, gwin_ref, gwout_ref,
    acts, wbuf, wt, acc, dgel, hid, gpre, terms, wpart, sib, zrecv, zsend,
    rs1, ssum, rs2, send_sem, recv_sem, w_sem, bulk_send, bulk_recv,
):
    R, T = outT_ref.shape
    H = win_ref.shape[1]
    G = 4 * R
    row, col, z = lax.axis_index("row"), lax.axis_index("col"), lax.axis_index("depth")
    y, x = lax.div(col, 4), lax.rem(col, 4)
    other = 1 - row

    def at(yy, xx):
        return lax.rem(yy + 4, 4) * 4 + lax.rem(xx + 4, 4)

    p_plus = (row, at(y + row, x + other), z)
    p_minus = (row, at(y - row, x - other), z)
    q_plus = (row, at(y + other, x + row), z)
    q_minus = (row, at(y - other, x - row), z)
    z_plus = (row, col, lax.rem(z + 1, 8))
    z_minus = (row, col, lax.rem(z + 7, 8))
    sibling = (other, col, z)
    partners = (p_plus, p_minus, q_plus, q_minus, z_plus, z_minus, sibling)

    def slot_of(block, core):
        dy = lax.rem(lax.div(block, 4) - y + 4, 4)
        dx = lax.rem(lax.rem(block, 4) - x + 4, 4)
        return dy * (4 - 3 * core) + dx * (1 + 3 * core)

    def rows_of(block, core):
        return pl.ds(pl.multiple_of(slot_of(block, core) * R, 32), R)

    copies = Copies(send_sem, recv_sem)

    local = []
    for w, src in ((0, win_ref), (1, wout_ref)):
        for i in range(8):
            block = row * 8 + i
            cp = pltpu.make_async_copy(
                src.at[pl.ds(i * R, R)], wbuf.at[w, rows_of(block, row)], w_sem.at[w]
            )
            cp.start()

    acts[0, 0:R, :] = tok_ref[...].astype(F32).T.astype(BF16)
    acts[1, 0:R, :] = grd_ref[...].astype(F32).T.astype(BF16)

    barrier = pltpu.get_barrier_semaphore()
    for dev in partners:
        pl.semaphore_signal(barrier, inc=1, device_id=dev, device_id_type=MESH)
    pl.semaphore_wait(barrier, len(partners))

    def shard(a, g, j, lo=0, hi=None):
        hi = R if hi is None else hi
        return acts.at[a, pl.ds((g * 4 + j) * R + lo, hi - lo)]

    got = {}
    half = R // 2

    def to_p(a):
        got[a, 0, 3] = [copies.start(shard(a, 0, 0), shard(a, 0, 3), p_plus)]
        got[a, 0, 1] = [copies.start(shard(a, 0, 0), shard(a, 0, 1), p_minus)]

    def to_q(a, j):
        got[a, 3, j] = [copies.start(shard(a, 0, j), shard(a, 3, j), q_plus)]
        got[a, 1, j] = [copies.start(shard(a, 0, j), shard(a, 1, j), q_minus)]

    def need(a, g, j):
        for cp in got.get((a, g, j), []):
            cp.wait_recv()
        got[a, g, j] = []

    def p_forward(a):
        need(a, 0, 3)
        first = copies.start(shard(a, 0, 3, 0, half), shard(a, 0, 2, 0, half), p_plus)
        to_q(a, 3)
        need(a, 0, 1)
        second = copies.start(shard(a, 0, 1, half, R), shard(a, 0, 2, half, R), p_minus)
        to_q(a, 1)
        got[a, 0, 2] = [first, second]

    def p_last(a):
        need(a, 0, 2)
        to_q(a, 2)

    def q_forward(a, step):
        j, k = (0, 2) if step == 0 else (1, 3)
        if step == 0:
            j, k = 0, 3
        else:
            j, k = 1, 2
        need(a, 3, j)
        got[a, 2, j] = [copies.start(shard(a, 3, j), shard(a, 2, j), q_plus)]
        need(a, 1, k)
        got[a, 2, k] = [copies.start(shard(a, 1, k), shard(a, 2, k), q_minus)]

    def group(a, g):
        for j in range(4):
            need(a, g, j)

    to_p(0)
    to_q(0, 0)
    for w, src in ((0, win_ref), (1, wout_ref)):
        for i in range(8):
            block = row * 8 + i
            pltpu.make_async_remote_copy(
                src_ref=src.at[pl.ds(i * R, R)],
                dst_ref=wbuf.at[w, rows_of(block, other)],
                send_sem=bulk_send.at[w],
                recv_sem=bulk_recv.at[w],
                device_id=sibling,
                device_id_type=MESH,
            ).start()
    to_p(1)
    p_forward(0)
    to_q(1, 0)
    p_last(0)

    def weights(w, src):
        pltpu.make_async_copy(src, wbuf.at[w, pl.ds(0, 8 * R)], w_sem.at[w]).wait()
        pltpu.make_async_remote_copy(
            src_ref=src, dst_ref=wbuf.at[w, pl.ds(0, 8 * R)], send_sem=bulk_send.at[w],
            recv_sem=bulk_recv.at[w], device_id=sibling, device_id_type=MESH,
        ).wait()

        @pl.loop(0, 4)
        def _(g):
            wt[w, g] = wbuf[w, pl.ds(pl.multiple_of(g * G, 128), G), :].T

    weights(0, win_ref)
    p_forward(1)
    p_last(1)
    q_forward(0, 0)
    q_forward(0, 1)
    weights(1, wout_ref)

    def project(a):
        for n, g in enumerate((0, 3, 1, 2)):
            group(a, g)
            part = nn(wt[a, g], acts[a, pl.ds(g * G, G), :])
            if n == 0:
                acc[...] = part
            else:
                acc[...] += part

    project(0)
    q_forward(1, 0)

    step = 32

    @pl.loop(0, H // step)
    def _(i):
        rows = pl.ds(pl.multiple_of(i * step, step), step)
        v = acc[rows, :]
        sq = v * v
        t = jnp.tanh(C0 * (v + C1 * (sq * v)))
        cdf = 0.5 * (1.0 + t)
        hid[rows, :] = (v * cdf).astype(BF16)
        dgel[rows, :] = cdf + (0.5 * C0) * v * (1.0 - t * t) * (1.0 + (3.0 * C1) * sq)

    q_forward(1, 1)

    def make_terms(a, w, src):
        @pl.loop(0, 4)
        def _(g):
            rows = pl.ds(pl.multiple_of(g * G, 128), G)
            terms[a, rows, :] = nn(wbuf[w, rows, :], src[...]).astype(BF16)

    def make_wpart(b, a, src):
        @pl.loop(0, 4)
        def _(g):
            rows = pl.ds(pl.multiple_of(g * G, 128), G)
            wpart[b, rows, :] = nt(acts[a, rows, :], src[...]).astype(BF16)

    def add(dst, srcs, rows, out=BF16):
        block = 32 if rows % 32 == 0 else 16

        @pl.loop(0, rows // block)
        def _(i):
            here = pl.multiple_of(i * block, block)
            total = None
            for ref, off in srcs:
                part = ref[pl.ds(pl.multiple_of(off + here, 16), block), :].astype(F32)
                total = part if total is None else total + part
            ref, off = dst
            ref[pl.ds(pl.multiple_of(off + here, 16), block), :] = total.astype(out)

    rs = {}

    def rs1a(a):
        t = terms.at[a]
        r = rs1.at[a]
        rs[a, "ra"] = copies.start(t.at[pl.ds(8 * R, 2 * R)], r.at[pl.ds(0, 2 * R)], q_plus)
        rs[a, "rb"] = copies.start(t.at[pl.ds(10 * R, 2 * R)], r.at[pl.ds(2 * R, 2 * R)], q_minus)
        rs[a, "rc1"] = copies.start(t.at[pl.ds(6 * R, 2 * R)], r.at[pl.ds(6 * R, 2 * R)], q_plus)
        rs[a, "rd0"] = copies.start(t.at[pl.ds(12 * R, 2 * R)], r.at[pl.ds(8 * R, 2 * R)], q_minus)

    def rs1b(a):
        t = terms.at[a]
        r = rs1.at[a]
        rs[a, "ra"].wait_recv()
        add((t, 4 * R), ((t, 4 * R), (r, 0)), 2 * R)
        rs[a, "rc0"] = copies.start(t.at[pl.ds(4 * R, 2 * R)], r.at[pl.ds(4 * R, 2 * R)], q_plus)
        rs[a, "rb"].wait_recv()
        add((t, 14 * R), ((t, 14 * R), (r, 2 * R)), 2 * R)
        rs[a, "rd1"] = copies.start(t.at[pl.ds(14 * R, 2 * R)], r.at[pl.ds(10 * R, 2 * R)], q_minus)

    def rs1c(a):
        t = terms.at[a]
        r = rs1.at[a]
        s = ssum.at[a]
        e = rs2.at[a]
        rs[a, "rc1"].wait_recv()
        rs[a, "rd1"].wait_recv()
        add((s, 2 * R), ((t, 2 * R), (r, 6 * R), (r, 10 * R)), 2 * R)
        rs[a, "re"] = copies.start(s.at[pl.ds(2 * R, half)], e.at[pl.ds(0, half)], p_plus)
        rs[a, "rf"] = copies.start(s.at[pl.ds(2 * R + half, half)], e.at[pl.ds(half, half)], p_minus)
        rs[a, "rc0"].wait_recv()
        rs[a, "rd0"].wait_recv()
        add((s, R), ((t, R), (r, 5 * R), (r, 9 * R)), R)

    def rs2b(a):
        s = ssum.at[a]
        e = rs2.at[a]
        rs[a, "re"].wait_recv()
        add((s, R), ((s, R), (e, 0)), half)
        rs[a, "rg"] = copies.start(s.at[pl.ds(R, R)], e.at[pl.ds(R, R)], p_plus)
        rs[a, "rf"].wait_recv()
        add((s, 3 * R + half), ((s, 3 * R + half), (e, half)), half)
        rs[a, "rh"] = copies.start(s.at[pl.ds(3 * R, R)], e.at[pl.ds(2 * R, R)], p_minus)

    def rs2c(a, out):
        t = terms.at[a]
        r = rs1.at[a]
        e = rs2.at[a]
        rs[a, "rg"].wait_recv()
        rs[a, "rh"].wait_recv()
        add((out, 0), ((t, 0), (r, 4 * R), (r, 8 * R), (e, R), (e, 2 * R)), R)

    finals = (gwout_ref, gwin_ref)
    zs = {}
    signs = (1, -1)
    orders = [(4 * d, -3 * d, 3 * d, -2 * d, 2 * d, -d, d, 0) for d in signs]

    def chunk(delta):
        return lax.rem(z + delta + 8, 8)

    def sib_send(b):
        for n, delta in enumerate(orders[b]):
            block = other * 8 + chunk(delta)
            zs[b, "sib", delta] = copies.start(
                wpart.at[b, rows_of(block, row)], sib.at[b, pl.ds(n * R, R)], sibling
            )

    def own(b, delta):
        zs[b, "sib", delta].wait_recv()
        n = orders[b].index(delta)
        mine = slot_of(row * 8 + chunk(delta), row) * R
        return ((wpart.at[b], mine), (sib.at[b], n * R))

    def ends(b, long):
        forward = (signs[b] > 0) == long
        return z_plus if forward else z_minus

    def z_step(b, long, s):
        hops, base = (4, 0) if long else (3, 4)
        delta = signs[b] * (4 - s) if long else -signs[b] * (3 - s)
        srcs = own(b, delta)
        if s > 0:
            zs[b, long, s - 1].wait_recv()
            srcs += ((zrecv.at[b], (base + s - 1) * R),)
        add((zsend.at[b], (base + s) * R), srcs, R)
        zs[b, long, s] = copies.start(
            zsend.at[b, pl.ds((base + s) * R, R)], zrecv.at[b, pl.ds((base + s) * R, R)], ends(b, long)
        )

    def z_both(b, s):
        z_step(b, True, s)
        if s < 3:
            z_step(b, False, s)

    def place(b, delta):
        return finals[b].at[pl.ds(pl.multiple_of(chunk(delta) * R, 32), R)]

    def z_final(b):
        srcs = own(b, 0)
        zs[b, True, 3].wait_recv()
        zs[b, False, 2].wait_recv()
        srcs += ((zrecv.at[b], 3 * R), (zrecv.at[b], 6 * R))
        add((zsend.at[b], 7 * R), srcs, R)
        mine = zsend.at[b, pl.ds(7 * R, R)]
        for long in (True, False):
            zs[b, "ag", long, 0] = copies.start(mine, place(b, 0), ends(b, long))
        zs[b, "own"] = pltpu.make_async_copy(mine, place(b, 0), w_sem.at[2 + b])
        zs[b, "own"].start()

    def z_gather(b, s):
        for long in (True, False):
            if s >= (4 if long else 3):
                continue
            delta = (-signs[b] if long else signs[b]) * s
            zs[b, "ag", long, s - 1].wait_recv()
            zs[b, "ag", long, s] = copies.start(place(b, delta), place(b, delta), ends(b, long))

    def z_end(b):
        zs[b, "own"].wait()
        zs[b, "ag", True, 3].wait_recv()
        zs[b, "ag", False, 2].wait_recv()

    make_terms(0, 1, hid)
    rs1a(0)
    for g in (0, 3, 1, 2):
        group(1, g)
    make_wpart(0, 1, hid)
    sib_send(0)
    project(1)
    z_both(0, 0)

    @pl.loop(0, H // step)
    def _(i):
        rows = pl.ds(pl.multiple_of(i * step, step), step)
        gpre[rows, :] = (acc[rows, :] * dgel[rows, :]).astype(BF16)

    make_wpart(1, 0, gpre)
    sib_send(1)
    rs1b(0)
    make_terms(1, 0, gpre)
    rs1a(1)
    z_both(1, 0)
    z_both(0, 1)
    rs1c(0)
    z_both(1, 1)
    z_both(0, 2)
    rs1b(1)
    rs2b(0)
    z_both(1, 2)
    z_both(0, 3)
    rs1c(1)
    rs2c(0, outT_ref)
    z_both(1, 3)
    z_final(0)
    rs2b(1)
    z_final(1)
    z_gather(0, 1)
    rs2c(1, gtokT_ref)
    z_gather(1, 1)
    z_gather(0, 2)
    z_gather(1, 2)
    z_gather(0, 3)
    z_gather(1, 3)
    z_end(0)
    z_end(1)
    for cp in copies.sent:
        cp.wait_send()


N_COPIES = 2 * 16 + 2 * 10 + 2 * (8 + 7 + 7)


def body(tokens_in, w_in, w_out, grad_out):
    T, R = tokens_in.shape
    H = w_in.shape[1]
    vmem = pl.BlockSpec(memory_space=pltpu.VMEM)
    hbm = pl.BlockSpec(memory_space=pl.ANY)
    outT, gtokT, g_in, g_out = pl.pallas_call(
        kernel,
        out_shape=(
            jax.ShapeDtypeStruct((R, T), BF16),
            jax.ShapeDtypeStruct((R, T), BF16),
            jax.ShapeDtypeStruct(w_in.shape, BF16),
            jax.ShapeDtypeStruct(w_out.shape, BF16),
        ),
        in_specs=[vmem, vmem, hbm, hbm],
        out_specs=(vmem, vmem, hbm, hbm),
        scratch_shapes=[
            pltpu.VMEM((2, 16 * R, T), BF16),
            pltpu.VMEM((2, 16 * R, H), BF16),
            pltpu.VMEM((2, 4, H, 4 * R), BF16),
            pltpu.VMEM((H, T), F32),
            pltpu.VMEM((H, T), F32),
            pltpu.VMEM((H, T), BF16),
            pltpu.VMEM((H, T), BF16),
            pltpu.VMEM((2, 16 * R, T), BF16),
            pltpu.VMEM((2, 16 * R, H), BF16),
            pltpu.VMEM((2, 8 * R, H), BF16),
            pltpu.VMEM((2, 7 * R, H), BF16),
            pltpu.VMEM((2, 8 * R, H), BF16),
            pltpu.VMEM((2, 12 * R, T), BF16),
            pltpu.VMEM((2, 4 * R, T), BF16),
            pltpu.VMEM((2, 3 * R, T), BF16),
            pltpu.SemaphoreType.DMA((N_COPIES,)),
            pltpu.SemaphoreType.DMA((N_COPIES,)),
            pltpu.SemaphoreType.DMA((4,)),
            pltpu.SemaphoreType.DMA((2,)),
            pltpu.SemaphoreType.DMA((2,)),
        ],
        compiler_params=pltpu.CompilerParams(
            collective_id=0, has_side_effects=True, vmem_limit_bytes=63 * 1024 * 1024
        ),
    )(tokens_in, grad_out, w_in, w_out)
    return outT.T, gtokT.T, g_in, g_out


def solution(mesh):
    placed = P(("row", "depth"), "col")
    weights = P("row", "col")
    return jax.shard_map(
        body,
        mesh=mesh,
        in_specs=(placed, weights, weights, placed),
        out_specs=(placed, placed, weights, weights),
        check_vma=False,
    )
```

time: 487 us -> 128 us (0.26)
  waiting for transfers between devices: 429 us -> 0 us
  Pallas kernels: 0 us -> 115 us
  matrix products: 26 us -> 0 us
  between operations: 14.2 us -> 0.64 us
    reduce_scatter x3 -> x0, waiting for transfers between devices: 245 us -> none  [the longest x1 84.2 us: body(): lax.psum_scatter(out_terms.astype(jnp.bfloat16), 'col', scatter_dimension...]
    all_gather x5 -> x0, waiting for transfers between devices: 181 us -> none  [the longest x1 54 us: body(): full_grads = lax.all_gather(grad_out, 'col', axis=1, tiled=True)]
    pallas_call x0 -> x1, Pallas kernels: none -> 115 us  [body(): pl.pallas_call(kernel, out_shape=(jax.ShapeDtypeStruct((R, T), BF16), jax...]
    dot_general x6 -> x0, matrix products: 26 us -> none  [the longest x2 11.2 us: times_transposed(): lax.dot_general(left, right, (((1,), (1,)), ((), ())), preferred_element_...]
    unnamed x11 -> x8, local copies, waits for them, and re-layouts: 9.92 us -> 10.7 us
  transfers between devices with their start and end apart: 8 -> 0, of which waited for: 8 -> 0; matrix products, arithmetic and copies ran while one was open for 4% -> 0% of each run, Pallas kernels for 0% -> 0%
where the time goes in v1:
time: 128 us; the launch traced here: 127 us
  Pallas kernels  115 us (90%)
  local copies, waits for them, and re-layouts  10.7 us (8%)
    pallas_call x1, Pallas kernels, body(): pl.pallas_call(kernel, out_shape=(jax.ShapeDtypeStruct((R, T), BF16), jax...  115 us
    unnamed x8, local copies, waits for them, and re-layouts  10.7 us

profile of v1, /device:TPU:1, one launch (start us, length us, event | category | flops | bytes accessed | tf_op | source)
XLA Modules:
  0.0 126.7 jit_solution(6635455248288684908)
XLA Ops:
  0.6 1.8 %copy.8.tok_ref = bf16[512,160]{1,0:T(8,128)(2,1)} copy(bf16[512,160]{0,1:T(8,128)(2,1)} %param.4) | data formatting | bytes 327680 | tf_op args[0]
  2.4 1.8 %copy.9.grd_ref = bf16[512,160]{1,0:T(8,128)(2,1)} copy(bf16[512,160]{0,1:T(8,128)(2,1)} %param.7) | data formatting | bytes 327680 | tf_op args[3]
  4.1 115.4 %shard_map.75 = (bf16[160,512]{1,0:T(8,128)(2,1)}, bf16[160,512]{1,0:T(8,128)(2,1)}, bf16[1280,640]{1,0:T(8,128)(2,1)}, bf16[1280,640]{1,0:T(8,128)(2,1)}) custom-call(bf16[512,160]{1,0:T(8,128)(2,1)} %copy.8.tok_ref, bf16[512,160]{1,0:T(8,128)(2,1)} %copy.9.grd_ref, bf16[1280,640]{1,0:T(8,128)(2,1)} %win_ref.1, bf16[1280,640]{1,0:T(8,128)(2,1)} %wout_ref.1), custom_call_target="tpu_custom_call" | custom-call | tf_op jit(solution)/shard_map/pallas_call | solution.py:412
  119.5 1.6 %copy.14 = bf16[512,160]{0,1:T(8,128)(2,1)} copy(bf16[512,160]{0,1:T(8,128)(2,1)} %bitcast.3) | data formatting | bytes 327680
  121.1 1.6 %copy.15 = bf16[512,160]{0,1:T(8,128)(2,1)} copy(bf16[512,160]{0,1:T(8,128)(2,1)} %bitcast.2) | data formatting | bytes 327680
  122.7 0.0 copy-start
  122.7 2.9 %copy.16 = bf16[1280,640]{1,0:T(8,128)(2,1)} copy(bf16[1280,640]{1,0:T(8,128)(2,1)} %get-tuple-element.18) | data formatting | bytes 3276800
  125.6 0.0 copy-done
  125.6 1.2 copy.17
Async XLA Ops:
  122.7 2.9 %copy-start = (bf16[1280,640]{1,0:T(8,128)(2,1)S(1)}, bf16[1280,640]{1,0:T(8,128)(2,1)}, u32[]{:S(2)}) copy-start(bf16[1280,640]{1,0:T(8,128)(2,1)} %get-tuple-element.19) | copy-start | bytes 4915204

commit v2 on v0

v2 whole, which is shorter than its diff:
```python
import functools

import jax
import jax.numpy as jnp
from jax import lax
from jax.experimental import pallas as pl
from jax.experimental.pallas import tpu as pltpu
from jax.sharding import PartitionSpec as P

MESH = pl.DeviceIdType.MESH
F32 = jnp.float32
BF16 = jnp.bfloat16
C0 = 0.7978845608028654
C1 = 0.044715


def nt(left, right):
    return lax.dot_general(left, right, (((1,), (1,)), ((), ())), preferred_element_type=F32)


def nn(left, right):
    return jnp.dot(left, right, preferred_element_type=F32)


class Local:
    def __init__(self, copy):
        self.wait_recv = copy.wait


class Copies:
    def __init__(self, send, recv):
        self.send, self.recv, self.count, self.sent = send, recv, 0, []

    def make(self, src, dst, device):
        k = self.count
        self.count += 1
        return pltpu.make_async_remote_copy(
            src_ref=src,
            dst_ref=dst,
            send_sem=self.send.at[k],
            recv_sem=self.recv.at[k],
            device_id=device,
            device_id_type=MESH,
        )

    def start(self, src, dst, device):
        copy = self.make(src, dst, device)
        copy.start()
        self.sent.append(copy)
        return copy


ORDER = (
    ((0, 0), (0, 1), (0, 3), (1, 0)),
    ((3, 0), (1, 1), (1, 3), (3, 1)),
    ((3, 3), (0, 2), (2, 0), (1, 2)),
    ((3, 2), (2, 1), (2, 3), (2, 2)),
)
FLAT = [pair for group in ORDER for pair in group]
SLOT = {pair: n for n, pair in enumerate(FLAT)}


def kernel(
    tok_ref, grd_ref, win_ref, wout_ref,
    outT_ref, gtokT_ref, gwin_ref, gwout_ref,
    acts, wbuf, wt, acc, dgel, hid, gpre, terms, wpart, sib, zrecv, fin,
    rs1, ssum, rs2, send_sem, recv_sem, w_sem, bulk_send, bulk_recv, o_sem, o_send, o_recv,
):
    R, T = outT_ref.shape
    H = win_ref.shape[1]
    G = 4 * R
    half = R // 2
    row, col, z = lax.axis_index("row"), lax.axis_index("col"), lax.axis_index("depth")
    y, x = lax.div(col, 4), lax.rem(col, 4)
    other = 1 - row

    def at(yy, xx):
        return lax.rem(yy + 4, 4) * 4 + lax.rem(xx + 4, 4)

    p_plus = (row, at(y + row, x + other), z)
    p_minus = (row, at(y - row, x - other), z)
    q_plus = (row, at(y + other, x + row), z)
    q_minus = (row, at(y - other, x - row), z)
    z_plus = (row, col, lax.rem(z + 1, 8))
    z_minus = (row, col, lax.rem(z + 7, 8))
    sibling = (other, col, z)
    partners = (p_plus, p_minus, q_plus, q_minus, z_plus, z_minus, sibling)

    barrier = pltpu.get_barrier_semaphore()
    for dev in partners:
        pl.semaphore_signal(barrier, inc=1, device_id=dev, device_id_type=MESH)

    copies = Copies(send_sem, recv_sem)
    owns = [
        pltpu.make_async_copy(src, acts.at[a, pl.ds(0, R)], w_sem.at[2 + a])
        for a, src in ((0, tok_ref), (1, grd_ref))
    ]
    for cp in owns:
        cp.start()

    def offset(g, j):
        one, two = SLOT[g, j], SLOT[j, g]
        if one == two:
            return one * R
        return pl.multiple_of((one + row * (two - one)) * R, 32)

    def shard(a, g, j, lo=0, hi=None):
        hi = R if hi is None else hi
        start = offset(g, j) + lo
        if not isinstance(start, int):
            start = pl.multiple_of(start, 16)
        return acts.at[a, pl.ds(start, hi - lo)]

    got = {}

    local = [Local(cp) for cp in owns]
    got.update({(0, 0, 0): [local[0]], (1, 0, 0): [local[1]]})

    def came(a, g, j, copy):
        got.setdefault((a, g, j), []).append(copy)

    def need(a, g, j):
        for cp in got.pop((a, g, j), []):
            cp.wait_recv()

    def to_p(a):
        src = (tok_ref, grd_ref)[a]
        came(a, 0, 3, copies.start(src, shard(a, 0, 3), p_plus))
        came(a, 0, 1, copies.start(src, shard(a, 0, 1), p_minus))

    def to_q(a, j):
        if j:
            need(a, 0, j)
        src = (tok_ref, grd_ref)[a] if j == 0 else shard(a, 0, j)
        came(a, 3, j, copies.start(src, shard(a, 3, j), q_plus))
        came(a, 1, j, copies.start(src, shard(a, 1, j), q_minus))

    def pf(a, g):
        need(a, 0, g)
        lo, hi, dev = (0, half, p_plus) if g == 3 else (half, R, p_minus)
        came(a, 0, 2, copies.start(shard(a, 0, g, lo, hi), shard(a, 0, 2, lo, hi), dev))

    def qf(a, g, j):
        need(a, g, j)
        came(a, 2, j, copies.start(shard(a, g, j), shard(a, 2, j), q_plus if g == 3 else q_minus))

    def group(a, n):
        if n == 0:
            need(a, 0, 0)
        for dy, dx in ORDER[n]:
            need(a, dy, dx)
            need(a, dx, dy)

    pl.semaphore_wait(barrier, len(partners))
    def wload():
        for dy in range(4):
            place_weights(dy)

    def place_weights(dy):
        yy = lax.rem(y + dy, 4)

        @pl.when(lax.div(yy, 2) == row)
        def _():
            for dx in range(4):
                n = SLOT[dy, dx]
                start = ((yy - 2 * row) * 4 + lax.rem(x + dx, 4)) * R
                block = pl.ds(pl.multiple_of(start, 32), R)
                for w, src in ((0, win_ref), (1, wout_ref)):
                    there = wbuf.at[w, pl.ds(n * R, R)]
                    pltpu.make_async_copy(src.at[block], there, w_sem.at[w]).start()
                    pltpu.make_async_remote_copy(
                        src_ref=src.at[block], dst_ref=there, send_sem=bulk_send.at[w],
                        recv_sem=bulk_recv.at[w], device_id=sibling, device_id_type=MESH,
                    ).start()

    def trans(w):
        src = (win_ref, wout_ref)[w]
        pltpu.make_async_copy(src, wbuf.at[w, pl.ds(0, 8 * R)], w_sem.at[w]).wait()
        pltpu.make_async_remote_copy(
            src_ref=src, dst_ref=wbuf.at[w, pl.ds(0, 8 * R)], send_sem=bulk_send.at[w],
            recv_sem=bulk_recv.at[w], device_id=sibling, device_id_type=MESH,
        ).wait()

        @pl.loop(0, 4)
        def _(g):
            wt[w, g] = wbuf[w, pl.ds(pl.multiple_of(g * G, 128), G), :].T

    def project(a, n):
        group(a, n)
        part = nn(wt[a, n], acts[a, pl.ds(n * G, G), :])
        if n == 0:
            acc[...] = part
        else:
            acc[...] += part

    def rows_at(n):
        return pl.ds(n * G if isinstance(n, int) else pl.multiple_of(n * G, 128), G)

    def make_terms(a, w, src, n):
        rows = rows_at(n)
        terms[a, rows, :] = nn(wbuf[w, rows, :], src[...]).astype(BF16)

    def make_wpart(b, a, src, n):
        rows = rows_at(n)
        wpart[b, rows, :] = nt(acts[a, rows, :], src[...]).astype(BF16)

    def add(dst, srcs, rows, out=BF16):
        block = 32 if rows % 32 == 0 else 16

        @pl.loop(0, rows // block)
        def _(i):
            here = pl.multiple_of(i * block, block)
            total = None
            for ref, off in srcs:
                part = ref[pl.ds(pl.multiple_of(off + here, 16), block), :].astype(F32)
                total = part if total is None else total + part
            ref, off = dst
            ref[pl.ds(pl.multiple_of(off + here, 16), block), :] = total.astype(out)

    rs = {}

    def piece(ref, start, rows):
        if not isinstance(start, int):
            start = pl.multiple_of(start, 16)
        return ref.at[pl.ds(start, rows)]

    def rs_a(a, g, j):
        t, r = terms.at[a], rs1.at[a]
        base, dev = {1: (4, q_plus), 3: (8, q_minus)}.get(g, (0, q_plus if j < 2 else q_minus))
        key = {1: "rc", 3: "rd"}.get(g, "ra")
        rs[a, key, j] = copies.start(piece(t, offset(g, j), R), piece(r, (base + j) * R, R), dev)

    def rs_b(a, g, j):
        t, r = terms.at[a], rs1.at[a]
        rs[a, "ra", j].wait_recv()
        add((t, offset(g, j)), ((t, offset(g, j)), (r, j * R)), R)
        rs_a(a, g, j)

    def rs_c(a, j):
        t, r, s, e = terms.at[a], rs1.at[a], ssum.at[a], rs2.at[a]
        rs[a, "rc", j].wait_recv()
        rs[a, "rd", j].wait_recv()
        add((s, j * R), ((t, offset(0, j)), (r, (4 + j) * R), (r, (8 + j) * R)), R)
        if j == 2:
            rs[a, "re"] = copies.start(piece(s, 2 * R, half), piece(e, 0, half), p_plus)
            rs[a, "rf"] = copies.start(piece(s, 2 * R + half, half), piece(e, half, half), p_minus)

    def rs_d(a, j):
        s, e = ssum.at[a], rs2.at[a]
        lo, key, dev = (0, "re", p_plus) if j == 1 else (half, "rf", p_minus)
        rs[a, key].wait_recv()
        add((s, j * R + lo), ((s, j * R + lo), (e, lo)), half)
        rs[a, "last", j] = copies.start(piece(s, j * R, R), piece(e, (1 + j // 2) * R, R), dev)

    def rs_e(a):
        t, r, e, out = terms.at[a], rs1.at[a], rs2.at[a], (outT_ref, gtokT_ref)[a]
        rs[a, "rc", 0].wait_recv()
        rs[a, "rd", 0].wait_recv()
        rs[a, "last", 1].wait_recv()
        rs[a, "last", 3].wait_recv()
        add((out, 0), ((t, 0), (r, 4 * R), (r, 8 * R), (e, R), (e, 2 * R)), R)

    finals = (gwout_ref, gwin_ref)
    zs = {}

    def sign(h):
        return 1 - 2 * h

    def order(h):
        d = sign(h)
        return (4 * d, -3 * d, 3 * d, -2 * d, 2 * d, -d, d, 0)

    def chunk(delta):
        return lax.rem(z + delta + 8, 8)

    def sib_send(b, h):
        for n, delta in enumerate(order(h)):
            start = h * 8 * R + other * G + chunk(delta) * half
            zs[b, h, "sib", delta] = copies.start(
                piece(wpart.at[b], start, half), piece(sib.at[b], h * G + n * half, half), sibling
            )

    def own(b, h, delta):
        zs[b, h, "sib", delta].wait_recv()
        n = order(h).index(delta)
        mine = pl.multiple_of(h * 8 * R + row * G + chunk(delta) * half, 16)
        return ((wpart.at[b], mine), (sib.at[b], h * G + n * half))

    def ends(h, long):
        return z_plus if (sign(h) > 0) == long else z_minus

    def z_one(b, h, long, n):
        base = h * 7 + (0 if long else 4)
        delta = sign(h) * (4 - n) if long else -sign(h) * (3 - n)
        srcs = own(b, h, delta)
        if n > 0:
            zs[b, h, long, n - 1].wait_recv()
            srcs += ((zrecv.at[b], (base + n - 1) * half),)
        add(srcs[0], srcs, half)
        zs[b, h, long, n] = copies.start(
            piece(*srcs[0], half), piece(zrecv.at[b], (base + n) * half, half), ends(h, long)
        )

    def place(b, h, delta):
        return piece(fin.at[b], h * G + chunk(delta) * half, half)

    def z_final(b, h):
        srcs = own(b, h, 0)
        zs[b, h, True, 3].wait_recv()
        zs[b, h, False, 2].wait_recv()
        base = h * 7
        srcs += ((zrecv.at[b], (base + 3) * half), (zrecv.at[b], (base + 6) * half))
        add((fin.at[b], pl.multiple_of(h * G + chunk(0) * half, 16)), srcs, half)
        for long in (True, False):
            zs[b, h, "ag", long, 0] = copies.start(place(b, h, 0), place(b, h, 0), ends(h, long))

    def z_gather(b, h, long, n):
        delta = (-sign(h) if long else sign(h)) * n
        zs[b, h, "ag", long, n - 1].wait_recv()
        zs[b, h, "ag", long, n] = copies.start(place(b, h, delta), place(b, h, delta), ends(h, long))

    def owner_of(h, j, core):
        one, two = FLAT[h * 8 + j], FLAT[h * 8 + 4 + j]
        dy, dx = (p + core * (q - p) for p, q in zip(one, two))
        yy = lax.rem(y + dy, 4)
        target = lax.div(yy, 2)
        start = ((yy - 2 * target) * 4 + lax.rem(x + dx, 4)) * R
        return target, pl.ds(pl.multiple_of(start, 32), R)

    def out_here(b, h, j, rows):
        n = (b * 2 + h) * 4 + j
        return pltpu.make_async_copy(piece(fin.at[b], h * G + j * R, R), finals[b].at[rows], o_sem.at[n])

    def out_there(b, h, j, rows):
        n = (b * 2 + h) * 4 + j
        return pltpu.make_async_remote_copy(
            src_ref=piece(fin.at[b], h * G + j * R, R), dst_ref=finals[b].at[rows],
            send_sem=o_send.at[n], recv_sem=o_recv.at[n], device_id=sibling, device_id_type=MESH,
        )

    def z_end(b, h):
        zs[b, h, "ag", True, 3].wait_recv()
        zs[b, h, "ag", False, 2].wait_recv()
        for j in range(4):
            target, rows = owner_of(h, j, row)
            pl.when(target == row)(lambda: out_here(b, h, j, rows).start())
            pl.when(target != row)(lambda: out_there(b, h, j, rows).start())

    def z_stored(b, h):
        for j in range(4):
            target, rows = owner_of(h, j, row)
            pl.when(target == row)(lambda: out_here(b, h, j, rows).wait())
            pl.when(target != row)(lambda: out_there(b, h, j, rows).wait_send())
            target, rows = owner_of(h, j, other)
            pl.when(target == row)(lambda: out_there(b, h, j, rows).wait_recv())

    def gelu():
        step = 32

        @pl.loop(0, H // step)
        def _(i):
            rows = pl.ds(pl.multiple_of(i * step, step), step)
            v = acc[rows, :]
            sq = v * v
            t = jnp.tanh(C0 * (v + C1 * (sq * v)))
            cdf = 0.5 * (1.0 + t)
            hid[rows, :] = (v * cdf).astype(BF16)
            dgel[rows, :] = cdf + (0.5 * C0) * v * (1.0 - t * t) * (1.0 + (3.0 * C1) * sq)

    def gelu_back():
        step = 32

        @pl.loop(0, H // step)
        def _(i):
            rows = pl.ds(pl.multiple_of(i * step, step), step)
            gpre[rows, :] = (acc[rows, :] * dgel[rows, :]).astype(BF16)

    def wpart_o(b, h):
        if b == 0:
            group(1, 2 * h)
            group(1, 2 * h + 1)
        make_wpart(b, 1 - b, (hid, gpre)[b], 2 * h + other)

    def wpart_m(b, h):
        make_wpart(b, 1 - b, (hid, gpre)[b], 2 * h + row)

    def terms_of(a, n):
        make_terms(a, 1 - a, (hid, gpre)[a], n)

    to_p(0)
    to_q(0, 0)
    wload()
    pf(0, 3)
    pf(0, 1)
    to_q(0, 3)
    to_q(0, 1)
    to_p(1)
    to_q(1, 0)
    qf(0, 3, 0)
    trans(0)
    to_q(0, 2)
    project(0, 0)
    qf(0, 1, 3)
    trans(1)
    qf(0, 3, 1)
    project(0, 1)
    pf(1, 3)
    pf(1, 1)
    to_q(1, 3)
    to_q(1, 1)
    qf(1, 3, 0)
    qf(0, 1, 2)
    project(0, 2)
    to_q(1, 2)
    qf(1, 1, 3)
    qf(1, 3, 1)
    project(0, 3)
    gelu()
    wpart_o(0, 0)
    sib_send(0, 0)
    qf(1, 1, 2)
    wpart_m(0, 0)
    project(1, 0)
    project(1, 1)
    terms_of(0, 3)
    z_one(0, 0, True, 0)
    z_one(0, 0, False, 0)
    terms_of(0, 2)
    terms_of(0, 1)
    terms_of(0, 0)
    rs_a(0, 2, 3)
    rs_a(0, 2, 2)
    rs_a(0, 2, 1)
    rs_a(0, 2, 0)
    rs_a(0, 3, 1)
    wpart_o(0, 1)
    sib_send(0, 1)
    wpart_m(0, 1)
    project(1, 2)
    project(1, 3)
    gelu_back()
    z_one(0, 0, True, 1)
    z_one(0, 0, False, 1)
    z_one(0, 1, True, 0)
    z_one(0, 1, False, 0)
    wpart_o(1, 0)
    sib_send(1, 0)
    wpart_m(1, 0)
    wpart_o(1, 1)
    sib_send(1, 1)
    wpart_m(1, 1)
    rs_b(0, 3, 3)
    z_one(1, 0, True, 0)
    rs_b(0, 3, 2)
    z_one(1, 0, False, 0)
    rs_b(0, 1, 1)
    rs_b(0, 1, 0)
    rs_a(0, 3, 0)
    rs_a(0, 1, 3)
    rs_a(0, 1, 2)
    terms_of(1, 3)
    terms_of(1, 2)
    z_one(0, 0, True, 2)
    z_one(0, 0, False, 2)
    z_one(1, 1, True, 0)
    terms_of(1, 1)
    z_one(1, 1, False, 0)
    terms_of(1, 0)
    rs_a(1, 2, 3)
    rs_a(1, 2, 2)
    rs_a(1, 2, 1)
    rs_a(1, 2, 0)
    rs_a(1, 3, 1)
    rs_a(1, 3, 0)
    rs_a(1, 1, 3)
    rs_a(1, 1, 2)
    z_one(0, 1, False, 1)
    z_one(0, 1, True, 1)
    rs_c(0, 1)
    z_one(1, 0, True, 1)
    z_one(1, 0, False, 1)
    rs_c(0, 3)
    z_one(0, 0, True, 3)
    rs_b(1, 3, 3)
    rs_c(0, 2)
    z_one(1, 1, False, 1)
    z_one(1, 1, True, 1)
    rs_b(1, 3, 2)
    rs_b(1, 1, 1)
    z_one(0, 1, False, 2)
    z_one(0, 1, True, 2)
    rs_b(1, 1, 0)
    z_one(1, 0, True, 2)
    z_one(1, 0, False, 2)
    rs_c(1, 3)
    z_final(0, 0)
    z_one(1, 1, True, 2)
    rs_d(0, 3)
    rs_d(0, 1)
    rs_c(1, 2)
    z_one(1, 1, False, 2)
    z_one(0, 1, True, 3)
    rs_c(1, 1)
    rs_d(1, 3)
    rs_e(0)
    z_one(1, 0, True, 3)
    z_gather(0, 0, False, 1)
    rs_d(1, 1)
    z_gather(0, 0, True, 1)
    z_one(1, 1, True, 3)
    rs_e(1)
    z_final(0, 1)
    z_final(1, 0)
    z_gather(0, 0, False, 2)
    z_gather(0, 0, True, 2)
    z_final(1, 1)
    z_gather(0, 1, False, 1)
    z_gather(0, 1, True, 1)
    z_gather(1, 0, True, 1)
    z_gather(1, 0, False, 1)
    z_gather(0, 0, True, 3)
    z_gather(1, 1, False, 1)
    z_gather(1, 1, True, 1)
    z_gather(0, 1, False, 2)
    z_gather(0, 1, True, 2)
    z_gather(1, 0, True, 2)
    z_gather(1, 0, False, 2)
    z_end(0, 0)
    z_gather(1, 1, True, 2)
    z_gather(1, 1, False, 2)
    z_gather(0, 1, True, 3)
    z_stored(0, 0)
    z_gather(1, 0, True, 3)
    z_gather(1, 1, True, 3)
    z_end(0, 1)
    z_end(1, 0)
    z_end(1, 1)
    z_stored(0, 1)
    z_stored(1, 0)
    z_stored(1, 1)
    for cp in copies.sent:
        cp.wait_send()


def settle(*refs):
    srcs, dsts, held, (into, out) = refs[:4], refs[4:8], refs[8:12], refs[12:]
    moves = []
    for src, dst, via in zip(srcs, dsts, held):
        parts = 1 if src.shape[0] < 512 else 4
        rows = src.shape[0] // parts
        for i in range(parts):
            here = pl.ds(i * rows, rows)
            n = len(moves)
            moves.append(
                (
                    pltpu.make_async_copy(src.at[here], via.at[here], into.at[n]),
                    pltpu.make_async_copy(via.at[here], dst.at[here], out.at[n]),
                )
            )
    for first, _ in moves:
        first.start()
    for first, second in moves:
        first.wait()
        second.start()
    for _, second in moves:
        second.wait()


N_COPIES = 2 * 16 + 2 * 16 + 4 * (8 + 7 + 7)


def body(tokens_in, w_in, w_out, grad_out):
    T, R = tokens_in.shape
    H = w_in.shape[1]
    tokT, grdT = tokens_in.T, grad_out.T
    vmem = pl.BlockSpec(memory_space=pltpu.VMEM)
    hbm = pl.BlockSpec(memory_space=pl.ANY)
    outT, gtokT, g_in, g_out = pl.pallas_call(
        kernel,
        out_shape=(
            jax.ShapeDtypeStruct((R, T), BF16),
            jax.ShapeDtypeStruct((R, T), BF16),
            jax.ShapeDtypeStruct(w_in.shape, BF16),
            jax.ShapeDtypeStruct(w_out.shape, BF16),
        ),
        in_specs=[hbm] * 4,
        out_specs=(vmem, vmem, hbm, hbm),
        scratch_shapes=[
            pltpu.VMEM((2, 16 * R, T), BF16),
            pltpu.VMEM((2, 16 * R, H), BF16),
            pltpu.VMEM((2, 4, H, 4 * R), BF16),
            pltpu.VMEM((H, T), F32),
            pltpu.VMEM((H, T), F32),
            pltpu.VMEM((H, T), BF16),
            pltpu.VMEM((H, T), BF16),
            pltpu.VMEM((2, 16 * R, T), BF16),
            pltpu.VMEM((2, 16 * R, H), BF16),
            pltpu.VMEM((2, 8 * R, H), BF16),
            pltpu.VMEM((2, 7 * R, H), BF16),
            pltpu.VMEM((2, 8 * R, H), BF16),
            pltpu.VMEM((2, 12 * R, T), BF16),
            pltpu.VMEM((2, 4 * R, T), BF16),
            pltpu.VMEM((2, 3 * R, T), BF16),
            pltpu.SemaphoreType.DMA((N_COPIES,)),
            pltpu.SemaphoreType.DMA((N_COPIES,)),
            pltpu.SemaphoreType.DMA((4,)),
            pltpu.SemaphoreType.DMA((2,)),
            pltpu.SemaphoreType.DMA((2,)),
            pltpu.SemaphoreType.DMA((16,)),
            pltpu.SemaphoreType.DMA((16,)),
            pltpu.SemaphoreType.DMA((16,)),
        ],
        compiler_params=pltpu.CompilerParams(
            collective_id=0, has_side_effects=True, vmem_limit_bytes=63 * 1024 * 1024
        ),
    )(tokT, grdT, w_in, w_out)
    arrays = (outT, gtokT, g_in, g_out)
    outT, gtokT, g_in, g_out = pl.pallas_call(
        settle,
        out_shape=tuple(jax.ShapeDtypeStruct(a.shape, BF16) for a in arrays),
        in_specs=[hbm] * 4,
        out_specs=(hbm,) * 4,
        scratch_shapes=[pltpu.VMEM(a.shape, BF16) for a in arrays] + [pltpu.SemaphoreType.DMA((10,))] * 2,
    )(*arrays)
    return outT.T, gtokT.T, g_in, g_out


def solution(mesh):
    placed = P(("row", "depth"), "col")
    weights = P("row", "col")
    return jax.shard_map(
        body,
        mesh=mesh,
        in_specs=(placed, weights, weights, placed),
        out_specs=(placed, placed, weights, weights),
        check_vma=False,
    )
```

time: 487 us -> 115 us (0.24)
  waiting for transfers between devices: 429 us -> 0 us
  Pallas kernels: 0 us -> 115 us
  matrix products: 26 us -> 0 us
  local copies, waits for them, and re-layouts: 13.8 us -> 0 us
  between operations: 14.2 us -> 0.64 us
    reduce_scatter x3 -> x0, waiting for transfers between devices: 245 us -> none  [the longest x1 84.2 us: body(): lax.psum_scatter(out_terms.astype(jnp.bfloat16), 'col', scatter_dimension...]
    all_gather x5 -> x0, waiting for transfers between devices: 181 us -> none  [the longest x1 54 us: body(): full_grads = lax.all_gather(grad_out, 'col', axis=1, tiled=True)]
    pallas_call x0 -> x2, Pallas kernels: none -> 115 us  [the longest x1 111 us: body(): pl.pallas_call(kernel, out_shape=(jax.ShapeDtypeStruct((R, T), BF16), jax...]
    dot_general x6 -> x0, matrix products: 26 us -> none  [the longest x2 11.2 us: times_transposed(): lax.dot_general(left, right, (((1,), (1,)), ((), ())), preferred_element_...]
    unnamed x11 -> x0, local copies, waits for them, and re-layouts: 9.92 us -> none
  transfers between devices with their start and end apart: 8 -> 0, of which waited for: 8 -> 0; matrix products, arithmetic and copies ran while one was open for 4% -> 0% of each run, Pallas kernels for 0% -> 0%
where the time goes in v2:
time: 115 us
  Pallas kernels  115 us (100%)
    pallas_call x1, Pallas kernels, body(): pl.pallas_call(kernel, out_shape=(jax.ShapeDtypeStruct((R, T), BF16), jax...  111 us
    pallas_call x1, Pallas kernels, body(): pl.pallas_call(settle, out_shape=tuple((jax.ShapeDtypeStruct(a.shape, BF1...  3.27 us

profile of v2, /device:TPU:1, one launch (start us, length us, event | category | flops | bytes accessed | tf_op | source)
XLA Modules:
  0.0 115.2 jit_solution(2543359567386659151)
XLA Ops:
  0.6 111.3 %shard_map.75 = (bf16[160,512]{1,0:T(8,128)(2,1)}, bf16[160,512]{1,0:T(8,128)(2,1)}, bf16[1280,640]{1,0:T(8,128)(2,1)}, bf16[1280,640]{1,0:T(8,128)(2,1)}) custom-call(bf16[160,512]{1,0:T(8,128)(2,1)} %bitcast.4, bf16[160,512]{1,0:T(8,128)(2,1)} %bitcast.5, bf16[1280,640]{1,0:T(8,128)(2,1)} %win_ref.1, bf16[1280,640]{1,0:T(8,128)(2,1)} %wout_ref.1), custom_call_target="tpu_custom_call" | custom-call | tf_op jit(solution)/shard_map/pallas_call | solution.py:578
  112.0 3.3 %shard_map.76 = (bf16[160,512]{1,0:T(8,128)(2,1)}, bf16[160,512]{1,0:T(8,128)(2,1)}, bf16[1280,640]{1,0:T(8,128)(2,1)}, bf16[1280,640]{1,0:T(8,128)(2,1)}) custom-call(bf16[160,512]{1,0:T(8,128)(2,1)} %get-tuple-element.12.refs_0_, bf16[160,512]{1,0:T(8,128)(2,1)} %get-tuple-element.13.refs_1_, bf16[1280,640]{1,0:T(8,128)(2,1)} %get-tuple-element.14.refs_2_, ...), custom_call_target="tpu_custom_call" | custom-call | tf_op jit(solution)/shard_map/pallas_call | solution.py:618

commit v3 on v2

--- a/solution.py
+++ b/solution.py
@@ -388,154 +388,154 @@
         make_terms(a, 1 - a, (hid, gpre)[a], n)
 
     to_p(0)
+    wload()
+    to_q(1, 0)
+    to_p(1)
+    to_q(0, 3)
+    pf(0, 3)
+    to_q(0, 1)
+    pf(0, 1)
     to_q(0, 0)
-    wload()
-    pf(0, 3)
-    pf(0, 1)
-    to_q(0, 3)
-    to_q(0, 1)
-    to_p(1)
-    to_q(1, 0)
+    to_q(0, 2)
+    pf(1, 1)
+    qf(0, 3, 1)
+    pf(1, 3)
+    qf(0, 1, 3)
+    to_q(1, 3)
+    qf(0, 1, 2)
     qf(0, 3, 0)
+    to_q(1, 1)
     trans(0)
-    to_q(0, 2)
+    qf(1, 3, 0)
+    trans(1)
+    to_q(1, 2)
     project(0, 0)
-    qf(0, 1, 3)
-    trans(1)
-    qf(0, 3, 1)
     project(0, 1)
-    pf(1, 3)
-    pf(1, 1)
-    to_q(1, 3)
-    to_q(1, 1)
-    qf(1, 3, 0)
-    qf(0, 1, 2)
     project(0, 2)
-    to_q(1, 2)
+    project(0, 3)
     qf(1, 1, 3)
-    qf(1, 3, 1)
-    project(0, 3)
     gelu()
     wpart_o(0, 0)
     sib_send(0, 0)
+    wpart_m(0, 0)
+    qf(1, 3, 1)
+    terms_of(0, 0)
+    z_one(0, 0, True, 0)
     qf(1, 1, 2)
-    wpart_m(0, 0)
+    z_one(0, 0, False, 0)
+    terms_of(0, 1)
+    terms_of(0, 3)
+    terms_of(0, 2)
+    rs_a(0, 2, 0)
+    rs_a(0, 3, 0)
     project(1, 0)
     project(1, 1)
-    terms_of(0, 3)
-    z_one(0, 0, True, 0)
-    z_one(0, 0, False, 0)
-    terms_of(0, 2)
-    terms_of(0, 1)
-    terms_of(0, 0)
-    rs_a(0, 2, 3)
+    z_one(0, 0, True, 1)
     rs_a(0, 2, 2)
-    rs_a(0, 2, 1)
-    rs_a(0, 2, 0)
-    rs_a(0, 3, 1)
+    z_one(0, 0, False, 1)
     wpart_o(0, 1)
     sib_send(0, 1)
     wpart_m(0, 1)
     project(1, 2)
+    z_one(0, 1, True, 0)
+    z_one(0, 1, False, 0)
     project(1, 3)
     gelu_back()
-    z_one(0, 0, True, 1)
-    z_one(0, 0, False, 1)
-    z_one(0, 1, True, 0)
-    z_one(0, 1, False, 0)
     wpart_o(1, 0)
+    z_one(0, 0, True, 2)
+    z_one(0, 0, False, 2)
     sib_send(1, 0)
     wpart_m(1, 0)
-    wpart_o(1, 1)
-    sib_send(1, 1)
-    wpart_m(1, 1)
-    rs_b(0, 3, 3)
+    terms_of(1, 3)
+    z_one(1, 0, False, 0)
     z_one(1, 0, True, 0)
-    rs_b(0, 3, 2)
-    z_one(1, 0, False, 0)
-    rs_b(0, 1, 1)
-    rs_b(0, 1, 0)
-    rs_a(0, 3, 0)
-    rs_a(0, 1, 3)
-    rs_a(0, 1, 2)
-    terms_of(1, 3)
-    terms_of(1, 2)
-    z_one(0, 0, True, 2)
-    z_one(0, 0, False, 2)
-    z_one(1, 1, True, 0)
-    terms_of(1, 1)
-    z_one(1, 1, False, 0)
-    terms_of(1, 0)
-    rs_a(1, 2, 3)
-    rs_a(1, 2, 2)
-    rs_a(1, 2, 1)
-    rs_a(1, 2, 0)
-    rs_a(1, 3, 1)
-    rs_a(1, 3, 0)
-    rs_a(1, 1, 3)
-    rs_a(1, 1, 2)
     z_one(0, 1, False, 1)
     z_one(0, 1, True, 1)
+    wpart_o(1, 1)
+    terms_of(1, 2)
+    sib_send(1, 1)
+    rs_a(0, 1, 2)
+    terms_of(1, 0)
+    rs_a(0, 2, 1)
+    wpart_m(1, 1)
+    z_one(1, 1, False, 0)
+    terms_of(1, 1)
+    rs_a(1, 1, 3)
+    rs_a(1, 2, 0)
+    z_one(1, 1, True, 0)
+    rs_a(1, 2, 3)
+    rs_a(0, 2, 3)
+    rs_b(0, 3, 2)
+    z_one(0, 0, True, 3)
+    z_one(1, 0, True, 1)
+    rs_a(1, 2, 2)
+    z_one(0, 1, True, 2)
+    z_one(1, 1, True, 1)
+    z_one(1, 1, False, 1)
+    z_one(1, 0, False, 1)
+    rs_a(1, 2, 1)
+    rs_a(0, 1, 3)
+    rs_b(0, 1, 0)
+    z_one(0, 1, False, 2)
+    rs_a(1, 3, 1)
+    z_one(1, 1, True, 2)
+    rs_a(0, 3, 1)
+    z_one(0, 1, True, 3)
+    z_one(1, 0, False, 2)
+    z_one(1, 0, True, 2)
+    rs_b(1, 3, 3)
+    z_final(0, 0)
+    z_one(1, 0, True, 3)
+    rs_b(1, 1, 1)
+    z_one(1, 1, True, 3)
+    rs_c(0, 2)
+    z_one(1, 1, False, 2)
+    rs_a(1, 1, 2)
+    z_final(0, 1)
+    z_gather(0, 0, True, 1)
+    z_final(1, 0)
+    rs_b(0, 1, 1)
+    rs_b(0, 3, 3)
+    z_gather(0, 1, True, 1)
+    rs_b(1, 3, 2)
+    z_gather(0, 1, False, 1)
+    z_final(1, 1)
+    z_gather(0, 0, False, 1)
+    rs_c(0, 3)
+    z_gather(1, 0, True, 1)
+    z_gather(0, 0, True, 2)
+    z_gather(0, 1, True, 2)
+    z_gather(0, 1, False, 2)
     rs_c(0, 1)
-    z_one(1, 0, True, 1)
-    z_one(1, 0, False, 1)
-    rs_c(0, 3)
-    z_one(0, 0, True, 3)
-    rs_b(1, 3, 3)
-    rs_c(0, 2)
-    z_one(1, 1, False, 1)
-    z_one(1, 1, True, 1)
-    rs_b(1, 3, 2)
-    rs_b(1, 1, 1)
-    z_one(0, 1, False, 2)
-    z_one(0, 1, True, 2)
     rs_b(1, 1, 0)
-    z_one(1, 0, True, 2)
-    z_one(1, 0, False, 2)
+    rs_a(1, 3, 0)
+    rs_d(0, 3)
+    z_gather(1, 1, True, 1)
+    rs_c(1, 2)
+    z_gather(1, 0, False, 1)
+    z_gather(0, 1, True, 3)
+    z_gather(1, 0, True, 2)
     rs_c(1, 3)
-    z_final(0, 0)
-    z_one(1, 1, True, 2)
-    rs_d(0, 3)
+    z_gather(1, 1, True, 2)
+    z_gather(1, 1, False, 1)
+    z_gather(0, 0, False, 2)
+    z_gather(0, 0, True, 3)
+    rs_c(1, 1)
     rs_d(0, 1)
-    rs_c(1, 2)
-    z_one(1, 1, False, 2)
-    z_one(0, 1, True, 3)
-    rs_c(1, 1)
+    z_gather(1, 0, True, 3)
+    rs_e(0)
     rs_d(1, 3)
-    rs_e(0)
-    z_one(1, 0, True, 3)
-    z_gather(0, 0, False, 1)
+    z_gather(1, 0, False, 2)
+    z_gather(1, 1, True, 3)
+    z_gather(1, 1, False, 2)
+    z_end(0, 1)
+    z_end(0, 0)
     rs_d(1, 1)
-    z_gather(0, 0, True, 1)
-    z_one(1, 1, True, 3)
+    z_stored(0, 1)
+    z_end(1, 0)
+    z_stored(0, 0)
+    z_end(1, 1)
     rs_e(1)
-    z_final(0, 1)
-    z_final(1, 0)
-    z_gather(0, 0, False, 2)
-    z_gather(0, 0, True, 2)
-    z_final(1, 1)
-    z_gather(0, 1, False, 1)
-    z_gather(0, 1, True, 1)
-    z_gather(1, 0, True, 1)
-    z_gather(1, 0, False, 1)
-    z_gather(0, 0, True, 3)
-    z_gather(1, 1, False, 1)
-    z_gather(1, 1, True, 1)
-    z_gather(0, 1, False, 2)
-    z_gather(0, 1, True, 2)
-    z_gather(1, 0, True, 2)
-    z_gather(1, 0, False, 2)
-    z_end(0, 0)
-    z_gather(1, 1, True, 2)
-    z_gather(1, 1, False, 2)
-    z_gather(0, 1, True, 3)
-    z_stored(0, 0)
-    z_gather(1, 0, True, 3)
-    z_gather(1, 1, True, 3)
-    z_end(0, 1)
-    z_end(1, 0)
-    z_end(1, 1)
-    z_stored(0, 1)
     z_stored(1, 0)
     z_stored(1, 1)
     for cp in copies.sent:
@@ -543,27 +543,18 @@
 
 
 def settle(*refs):
-    srcs, dsts, held, (into, out) = refs[:4], refs[4:8], refs[8:12], refs[12:]
+    sems = refs[8]
     moves = []
-    for src, dst, via in zip(srcs, dsts, held):
+    for src, dst in zip(refs[:4], refs[4:8]):
         parts = 1 if src.shape[0] < 512 else 4
         rows = src.shape[0] // parts
         for i in range(parts):
             here = pl.ds(i * rows, rows)
-            n = len(moves)
-            moves.append(
-                (
-                    pltpu.make_async_copy(src.at[here], via.at[here], into.at[n]),
-                    pltpu.make_async_copy(via.at[here], dst.at[here], out.at[n]),
-                )
-            )
-    for first, _ in moves:
-        first.start()
-    for first, second in moves:
-        first.wait()
-        second.start()
-    for _, second in moves:
-        second.wait()
+            moves.append(pltpu.make_async_copy(src.at[here], dst.at[here], sems.at[len(moves)]))
+    for move in moves:
+        move.start()
+    for move in moves:
+        move.wait()
 
 
 N_COPIES = 2 * 16 + 2 * 16 + 4 * (8 + 7 + 7)
@@ -578,13 +569,13 @@
     outT, gtokT, g_in, g_out = pl.pallas_call(
         kernel,
         out_shape=(
-            jax.ShapeDtypeStruct((R, T), BF16),
-            jax.ShapeDtypeStruct((R, T), BF16),
-            jax.ShapeDtypeStruct(w_in.shape, BF16),
-            jax.ShapeDtypeStruct(w_out.shape, BF16),
+            pltpu.VMEM((R, T), BF16),
+            pltpu.VMEM((R, T), BF16),
+            pltpu.VMEM(w_in.shape, BF16),
+            pltpu.VMEM(w_out.shape, BF16),
         ),
         in_specs=[hbm] * 4,
-        out_specs=(vmem, vmem, hbm, hbm),
+        out_specs=(vmem,) * 4,
         scratch_shapes=[
             pltpu.VMEM((2, 16 * R, T), BF16),
             pltpu.VMEM((2, 16 * R, H), BF16),
@@ -611,16 +602,17 @@
             pltpu.SemaphoreType.DMA((16,)),
         ],
         compiler_params=pltpu.CompilerParams(
-            collective_id=0, has_side_effects=True, vmem_limit_bytes=63 * 1024 * 1024
+            collective_id=0, has_side_effects=True, vmem_limit_bytes=54 * 1024 * 1024
         ),
     )(tokT, grdT, w_in, w_out)
-    arrays = (outT, gtokT, g_in, g_out)
+    arrays = tuple(pltpu.with_memory_space_constraint(a, pltpu.VMEM) for a in (outT, gtokT, g_in, g_out))
     outT, gtokT, g_in, g_out = pl.pallas_call(
         settle,
         out_shape=tuple(jax.ShapeDtypeStruct(a.shape, BF16) for a in arrays),
-        in_specs=[hbm] * 4,
+        in_specs=[vmem] * 4,
         out_specs=(hbm,) * 4,
-        scratch_shapes=[pltpu.VMEM(a.shape, BF16) for a in arrays] + [pltpu.SemaphoreType.DMA((10,))] * 2,
+        scratch_shapes=[pltpu.SemaphoreType.DMA((10,))],
+        compiler_params=pltpu.CompilerParams(vmem_limit_bytes=4 * 1024 * 1024),
     )(*arrays)
     return outT.T, gtokT.T, g_in, g_out
 

time: 115 us -> 111 us (0.965)
  Pallas kernels: 115 us -> 110 us
    pallas_call x1, Pallas kernels: 111 us -> 108 us  [body(): pl.pallas_call(kernel, out_shape=(pltpu.VMEM((R, T), BF16), pltpu.VMEM((R...]
    pallas_call x1, Pallas kernels: 3.27 us -> 1.89 us  [body(): pl.pallas_call(settle, out_shape=tuple((jax.ShapeDtypeStruct(a.shape, BF1...]
where the time goes in v3:
time: 111 us
  Pallas kernels  110 us (99%)
    pallas_call x1, Pallas kernels, body(): pl.pallas_call(kernel, out_shape=(pltpu.VMEM((R, T), BF16), pltpu.VMEM((R...  108 us

profile of v3, /device:TPU:1, one launch (start us, length us, event | category | flops | bytes accessed | tf_op | source)
XLA Modules:
  0.0 110.6 jit_solution(15321689023572485938)
XLA Ops:
  0.6 108.0 %shard_map.75 = (bf16[160,512]{1,0:T(8,128)(2,1)S(1)}, bf16[160,512]{1,0:T(8,128)(2,1)S(1)}, bf16[1280,640]{1,0:T(8,128)(2,1)S(1)}, bf16[1280,640]{1,0:T(8,128)(2,1)S(1)}) custom-call(bf16[160,512]{1,0:T(8,128)(2,1)} %bitcast.4, bf16[160,512]{1,0:T(8,128)(2,1)} %bitcast.5, bf16[1280,640]{1,0:T(8,128)(2,1)} %win_ref.1, bf16[1280,640]{1,0:T(8,128)(2,1)} %wout_ref.1), custom_call_target="tpu_custom_call" | custom-call | tf_op jit(solution)/shard_map/pallas_call | solution.py:569
  108.7 1.9 %shard_map.76 = (bf16[160,512]{1,0:T(8,128)(2,1)}, bf16[160,512]{1,0:T(8,128)(2,1)}, bf16[1280,640]{1,0:T(8,128)(2,1)}, bf16[1280,640]{1,0:T(8,128)(2,1)}) custom-call(bf16[160,512]{1,0:T(8,128)(2,1)S(1)} %get-tuple-element.12.refs_0_, bf16[160,512]{1,0:T(8,128)(2,1)S(1)} %get-tuple-element.13.refs_1_, bf16[1280,640]{1,0:T(8,128)(2,1)S(1)} %get-tuple-element.14.refs_2_, ...), custom_call_target="tpu_custom_call" | custom-call | tf_op jit(solution)/shard_map/pallas_call | solution.py:609

commit v4 on v3

--- a/solution.py
+++ b/solution.py
@@ -48,6 +48,10 @@
         copy.start()
         self.sent.append(copy)
         return copy
+
+    def flush(self, keep):
+        while len(self.sent) > keep:
+            self.sent.pop(0).wait_send()
 
 
 ORDER = (
@@ -124,14 +128,14 @@
             cp.wait_recv()
 
     def to_p(a):
-        src = (tok_ref, grd_ref)[a]
+        need(a, 0, 0)
+        src = shard(a, 0, 0)
         came(a, 0, 3, copies.start(src, shard(a, 0, 3), p_plus))
         came(a, 0, 1, copies.start(src, shard(a, 0, 1), p_minus))
 
     def to_q(a, j):
-        if j:
-            need(a, 0, j)
-        src = (tok_ref, grd_ref)[a] if j == 0 else shard(a, 0, j)
+        need(a, 0, j)
+        src = shard(a, 0, j)
         came(a, 3, j, copies.start(src, shard(a, 3, j), q_plus))
         came(a, 1, j, copies.start(src, shard(a, 1, j), q_minus))
 
@@ -388,158 +392,159 @@
         make_terms(a, 1 - a, (hid, gpre)[a], n)
 
     to_p(0)
-    wload()
+    to_q(0, 0)
     to_q(1, 0)
     to_p(1)
-    to_q(0, 3)
-    pf(0, 3)
+    qf(0, 3, 0)
     to_q(0, 1)
     pf(0, 1)
-    to_q(0, 0)
+    pf(0, 3)
+    to_q(0, 3)
+    wload()
+    pf(1, 3)
+    pf(1, 1)
     to_q(0, 2)
-    pf(1, 1)
+    to_q(1, 1)
+    qf(0, 1, 3)
+    trans(0)
     qf(0, 3, 1)
-    pf(1, 3)
-    qf(0, 1, 3)
+    qf(0, 1, 2)
     to_q(1, 3)
-    qf(0, 1, 2)
-    qf(0, 3, 0)
-    to_q(1, 1)
-    trans(0)
-    qf(1, 3, 0)
+    project(0, 0)
     trans(1)
+    qf(1, 3, 1)
     to_q(1, 2)
-    project(0, 0)
     project(0, 1)
     project(0, 2)
     project(0, 3)
+    gelu()
     qf(1, 1, 3)
-    gelu()
     wpart_o(0, 0)
     sib_send(0, 0)
     wpart_m(0, 0)
-    qf(1, 3, 1)
-    terms_of(0, 0)
+    qf(1, 3, 0)
+    qf(1, 1, 2)
+    terms_of(0, 2)
     z_one(0, 0, True, 0)
-    qf(1, 1, 2)
     z_one(0, 0, False, 0)
     terms_of(0, 1)
-    terms_of(0, 3)
-    terms_of(0, 2)
-    rs_a(0, 2, 0)
-    rs_a(0, 3, 0)
     project(1, 0)
     project(1, 1)
+    terms_of(0, 3)
+    terms_of(0, 0)
+    wpart_o(0, 1)
     z_one(0, 0, True, 1)
-    rs_a(0, 2, 2)
     z_one(0, 0, False, 1)
-    wpart_o(0, 1)
     sib_send(0, 1)
+    project(1, 2)
+    project(1, 3)
     wpart_m(0, 1)
-    project(1, 2)
     z_one(0, 1, True, 0)
     z_one(0, 1, False, 0)
-    project(1, 3)
     gelu_back()
+    wpart_o(1, 1)
+    sib_send(1, 1)
+    rs_a(0, 2, 0)
+    z_one(0, 0, True, 2)
+    wpart_m(1, 1)
+    z_one(1, 1, True, 0)
+    z_one(0, 1, True, 1)
+    z_one(1, 1, False, 0)
     wpart_o(1, 0)
-    z_one(0, 0, True, 2)
-    z_one(0, 0, False, 2)
     sib_send(1, 0)
     wpart_m(1, 0)
+    rs_a(0, 2, 1)
+    z_one(0, 0, False, 2)
+    z_one(0, 1, False, 1)
+    rs_a(0, 2, 2)
     terms_of(1, 3)
+    z_one(0, 0, True, 3)
+    z_one(1, 0, True, 0)
+    terms_of(1, 1)
+    z_one(0, 1, True, 2)
+    rs_a(0, 3, 0)
+    terms_of(1, 2)
+    terms_of(1, 0)
+    rs_a(1, 1, 3)
+    rs_a(1, 2, 3)
     z_one(1, 0, False, 0)
-    z_one(1, 0, True, 0)
-    z_one(0, 1, False, 1)
-    z_one(0, 1, True, 1)
-    wpart_o(1, 1)
-    terms_of(1, 2)
-    sib_send(1, 1)
+    z_one(0, 1, False, 2)
+    z_final(0, 0)
+    rs_a(1, 2, 2)
+    rs_a(1, 1, 2)
+    z_one(1, 1, False, 1)
+    rs_a(0, 3, 1)
+    rs_a(0, 2, 3)
+    rs_b(0, 1, 0)
+    rs_b(0, 1, 1)
     rs_a(0, 1, 2)
-    terms_of(1, 0)
-    rs_a(0, 2, 1)
-    wpart_m(1, 1)
-    z_one(1, 1, False, 0)
-    terms_of(1, 1)
-    rs_a(1, 1, 3)
+    z_one(0, 1, True, 3)
+    z_one(1, 1, True, 1)
+    z_gather(0, 0, False, 1)
+    z_one(1, 0, True, 1)
+    rs_b(1, 3, 3)
+    z_one(1, 0, False, 1)
     rs_a(1, 2, 0)
-    z_one(1, 1, True, 0)
-    rs_a(1, 2, 3)
-    rs_a(0, 2, 3)
+    z_final(0, 1)
+    rs_a(1, 3, 1)
+    rs_a(0, 1, 3)
+    rs_b(1, 3, 2)
+    z_one(1, 1, False, 2)
+    z_one(1, 1, True, 2)
+    rs_a(1, 2, 1)
+    z_one(1, 0, True, 2)
+    z_gather(0, 0, True, 1)
     rs_b(0, 3, 2)
-    z_one(0, 0, True, 3)
-    z_one(1, 0, True, 1)
-    rs_a(1, 2, 2)
-    z_one(0, 1, True, 2)
-    z_one(1, 1, True, 1)
-    z_one(1, 1, False, 1)
-    z_one(1, 0, False, 1)
-    rs_a(1, 2, 1)
-    rs_a(0, 1, 3)
-    rs_b(0, 1, 0)
-    z_one(0, 1, False, 2)
-    rs_a(1, 3, 1)
-    z_one(1, 1, True, 2)
-    rs_a(0, 3, 1)
-    z_one(0, 1, True, 3)
+    z_gather(0, 0, False, 2)
+    rs_b(0, 3, 3)
+    rs_c(1, 3)
+    rs_b(1, 1, 0)
     z_one(1, 0, False, 2)
-    z_one(1, 0, True, 2)
-    rs_b(1, 3, 3)
-    z_final(0, 0)
+    rs_c(0, 1)
     z_one(1, 0, True, 3)
+    z_one(1, 1, True, 3)
+    z_gather(0, 0, True, 2)
     rs_b(1, 1, 1)
-    z_one(1, 1, True, 3)
     rs_c(0, 2)
-    z_one(1, 1, False, 2)
-    rs_a(1, 1, 2)
-    z_final(0, 1)
-    z_gather(0, 0, True, 1)
     z_final(1, 0)
-    rs_b(0, 1, 1)
-    rs_b(0, 3, 3)
+    z_final(1, 1)
+    rs_c(1, 2)
     z_gather(0, 1, True, 1)
-    rs_b(1, 3, 2)
+    rs_d(0, 1)
+    z_gather(0, 0, True, 3)
+    rs_c(0, 3)
+    rs_c(1, 1)
+    rs_d(0, 3)
     z_gather(0, 1, False, 1)
-    z_final(1, 1)
-    z_gather(0, 0, False, 1)
-    rs_c(0, 3)
     z_gather(1, 0, True, 1)
-    z_gather(0, 0, True, 2)
+    rs_a(1, 3, 0)
+    rs_d(1, 3)
+    z_gather(1, 1, True, 1)
     z_gather(0, 1, True, 2)
+    rs_d(1, 1)
+    copies.flush(40)
+    z_end(0, 0)
+    z_gather(1, 1, False, 1)
+    z_gather(1, 0, False, 1)
+    z_gather(1, 1, True, 2)
+    z_gather(1, 0, True, 2)
+    rs_e(0)
+    z_stored(0, 0)
+    rs_e(1)
+    z_gather(0, 1, True, 3)
     z_gather(0, 1, False, 2)
-    rs_c(0, 1)
-    rs_b(1, 1, 0)
-    rs_a(1, 3, 0)
-    rs_d(0, 3)
-    z_gather(1, 1, True, 1)
-    rs_c(1, 2)
-    z_gather(1, 0, False, 1)
-    z_gather(0, 1, True, 3)
-    z_gather(1, 0, True, 2)
-    rs_c(1, 3)
-    z_gather(1, 1, True, 2)
-    z_gather(1, 1, False, 1)
-    z_gather(0, 0, False, 2)
-    z_gather(0, 0, True, 3)
-    rs_c(1, 1)
-    rs_d(0, 1)
+    z_gather(1, 0, False, 2)
     z_gather(1, 0, True, 3)
-    rs_e(0)
-    rs_d(1, 3)
-    z_gather(1, 0, False, 2)
     z_gather(1, 1, True, 3)
     z_gather(1, 1, False, 2)
     z_end(0, 1)
-    z_end(0, 0)
-    rs_d(1, 1)
+    z_end(1, 0)
     z_stored(0, 1)
-    z_end(1, 0)
-    z_stored(0, 0)
+    copies.flush(8)
     z_end(1, 1)
-    rs_e(1)
     z_stored(1, 0)
     z_stored(1, 1)
-    for cp in copies.sent:
-        cp.wait_send()
+    copies.flush(0)
 
 
 def settle(*refs):

time: 111 us -> 111 us (level)
  no operation moved by 1% of the time
where the time goes in v4:
time: 111 us; the launch traced here: 110 us
  Pallas kernels  110 us (99%)
    pallas_call x1, Pallas kernels, body(): pl.pallas_call(kernel, out_shape=(pltpu.VMEM((R, T), BF16), pltpu.VMEM((R...  108 us

profile of v4, /device:TPU:1, one launch (start us, length us, event | category | flops | bytes accessed | tf_op | source)
XLA Modules:
  0.0 110.5 jit_solution(4685333302451642767)
XLA Ops:
  0.6 107.9 %shard_map.75 = (bf16[160,512]{1,0:T(8,128)(2,1)S(1)}, bf16[160,512]{1,0:T(8,128)(2,1)S(1)}, bf16[1280,640]{1,0:T(8,128)(2,1)S(1)}, bf16[1280,640]{1,0:T(8,128)(2,1)S(1)}) custom-call(bf16[160,512]{1,0:T(8,128)(2,1)} %bitcast.4, bf16[160,512]{1,0:T(8,128)(2,1)} %bitcast.5, bf16[1280,640]{1,0:T(8,128)(2,1)} %win_ref.1, bf16[1280,640]{1,0:T(8,128)(2,1)} %wout_ref.1), custom_call_target="tpu_custom_call" | custom-call | tf_op jit(solution)/shard_map/pallas_call | solution.py:574
  108.6 1.9 %shard_map.76 = (bf16[160,512]{1,0:T(8,128)(2,1)}, bf16[160,512]{1,0:T(8,128)(2,1)}, bf16[1280,640]{1,0:T(8,128)(2,1)}, bf16[1280,640]{1,0:T(8,128)(2,1)}) custom-call(bf16[160,512]{1,0:T(8,128)(2,1)S(1)} %get-tuple-element.12.refs_0_, bf16[160,512]{1,0:T(8,128)(2,1)S(1)} %get-tuple-element.13.refs_1_, bf16[1280,640]{1,0:T(8,128)(2,1)S(1)} %get-tuple-element.14.refs_2_, ...), custom_call_target="tpu_custom_call" | custom-call | tf_op jit(solution)/shard_map/pallas_call | solution.py:614
